TPU v7x, 32 devices: a whole 2x2x4 slice. The times are simulated.
32 devices in a mesh: batch: 8 (over z, y), hidden: 4 (over x, core).
Axes of the slice: x: 2, y: 2, z: 4, core: 2. Of those that a mesh axis runs over, the one named last changes fastest.
Arguments:
- layer_input: float32 [2, 768, 8192], P(None, 'hidden', 'batch'), may hold values from -6 to 6
- gain_first: float32 [768], P('hidden'), may hold values from 0.5 to 1.5
- shift_first: float32 [768], P('hidden'), may hold values from -2 to 2
- weight_in: float32 [768, 3072], P(None, 'hidden'), may hold values from -0.21875 to 0.21875
- bias_in: float32 [3072], P('hidden'), may hold values from -2 to 2
- weight_out: float32 [3072, 768], P('hidden'), may hold values from -0.109375 to 0.109375
- bias_out: float32 [768], P('hidden'), may hold values from -2 to 2
- gain_second: float32 [768], P('hidden'), may hold values from 0.5 to 1.5
- shift_second: float32 [768], P('hidden'), may hold values from -2 to 2
- cotangent: float32 [2, 768, 8192], P(None, 'hidden', 'batch'), may hold values from -6 to 6
- live_counts: int32 [8], P('batch'), may hold values from 1 to 2, as said below
Outputs:
- layer_output: float32 [2, 768, 8192], P(None, 'hidden', 'batch')
- input_grad: float32 [2, 768, 8192], P(None, 'hidden', 'batch')
- gain_first_grad: float32 [768], P('hidden')
- shift_first_grad: float32 [768], P('hidden')
- weight_in_grad: float32 [768, 3072], P(None, 'hidden')
- bias_in_grad: float32 [3072], P('hidden')
- weight_out_grad: float32 [3072, 768], P('hidden')
- bias_out_grad: float32 [768], P('hidden')
- gain_second_grad: float32 [768], P('hidden')
- shift_second_grad: float32 [768], P('hidden')
Inputs may be any that keep to these rules, and one draw needn't show every extreme that they name: `live_counts`: entries are equal within each aligned block of 4 batch indices (one batch group); each group holds 1 to 2 live sequences in its first slots; some group has all 2 slots live.
All inputs are finite; a program needn't handle non-finite values.
Results may differ from a plain program's by a relative error of at most 0.008.
Values may be sent and summed in bfloat16 or wider, within the bound.
A program may use at most 128 MiB of HBM per device.

v0:
```python
import functools
import math

import jax
import jax.numpy as jnp
import ml_dtypes
import numpy as np
from jax import lax
from jax.experimental import pallas as pl
from jax.experimental.pallas import tpu as pltpu
from jax.sharding import PartitionSpec as P

SPLIT = 4
HOLD = 4
EPS = 1e-06
FINE = 64
LOW = jnp.bfloat16
F32 = jnp.float32
MESH = pl.DeviceIdType.MESH
VMEM_LIMIT = 63 * 2**20


def dot(left, right):
    return jnp.dot(left, right, preferred_element_type=F32)


def dot_rows(left, right):
    return lax.dot_general(left, right, (((1,), (1,)), ((), ())), preferred_element_type=F32)


@functools.cache
def sequence_tables(length, split):
    column = np.arange(length)
    coarse = 2 * np.pi * ((FINE * np.arange(length // FINE)[:, None] * column) % length) / length
    fine = 2 * np.pi * ((np.arange(FINE)[:, None] * column) % length) / length
    factor = 1 / math.sqrt(length)
    whole = np.stack([np.cos(coarse), np.sin(coarse), factor * np.cos(fine), factor * np.sin(fine)])
    return np.ascontiguousarray(
        whole.reshape(4, FINE, split, length // split).transpose(2, 0, 1, 3).astype(np.float32)
    )


@functools.cache
def feature_tables(width, parts):
    index = np.arange(width)
    angle = 2 * np.pi * ((index[:, None] * index) % width) / width
    factor = 1 / math.sqrt(width)
    cos = (np.cos(angle) * factor).astype(np.float32).astype(ml_dtypes.bfloat16)
    sin = (np.sin(angle) * factor).astype(np.float32).astype(ml_dtypes.bfloat16)
    part = width // parts
    pad = part + 16
    forward = np.zeros((parts, parts, part, 2 * part), ml_dtypes.bfloat16)
    backward = np.zeros((parts, pad, width), ml_dtypes.bfloat16)
    order = np.zeros((parts, part, pad), ml_dtypes.bfloat16)
    for h in range(parts):
        chip = slice((h // 2) * 2 * part, (h // 2 + 1) * 2 * part)
        forward[h] = (cos if h % 2 == 0 else -sin)[:, chip].reshape(parts, part, 2 * part)
        first = (h // 2) * part
        backward[h, : part + 1] = (cos, sin)[h % 2][first : first + part + 1]
        for i in range(part):
            order[h, i, i if h in (0, 3) else part - i] = 1
    return forward, backward, order


class Place:
    def __init__(self, bits):
        h = lax.axis_index("hidden")
        b = lax.axis_index("batch")
        self.h, self.b = h, b
        self.c = lax.rem(h, 2)
        self.x = lax.div(h, 2)
        self.hc = h + 1 - 2 * self.c
        self.hx = lax.rem(h + 2, 4)
        self.hd = lax.rem(self.hc + 2, 4)
        self.p = lax.rem(b, 4)
        self.bit = [lax.rem(lax.div(b, 2**k), 2) for k in range(bits)]
        self.py = self.p + 1 - 2 * self.bit[0]
        self.pz = lax.rem(self.p + 2, 4)
        self.pd = lax.rem(self.py + 2, 4)
        self.core = {"hidden": self.hc}
        self.side = {"hidden": self.hx}
        self.cross = {"hidden": self.hd}
        self.flip = [{"batch": b + 2**k - 2 ** (k + 1) * self.bit[k]} for k in range(bits)]
        self.ydev, self.zdev = self.flip[:2]


class Links:
    def __init__(self, send, recv, near):
        self.send, self.recv, self.near = send, recv, near
        self.used, self.fetched, self.open = 0, 0, []

    def describe(self, src, dst, device):
        i = self.used
        self.used += 1
        return pltpu.make_async_remote_copy(
            src_ref=src,
            dst_ref=dst,
            send_sem=self.send.at[i],
            recv_sem=self.recv.at[i],
            device_id=device,
            device_id_type=MESH,
        )

    def copy(self, src, dst, device):
        made = self.describe(src, dst, device)
        made.start()
        self.open.append(made)
        return made

    def settle(self, some):
        for made in some:
            made.wait_send()
            self.drop(made)

    def drop(self, made):
        self.open = [other for other in self.open if other is not made]

    def fetch(self, src, dst):
        made = pltpu.make_async_copy(src, dst, self.near.at[self.fetched])
        self.fetched += 1
        made.start()
        return made


def greet(devices):
    barrier = pltpu.get_barrier_semaphore()
    for device in devices:
        pl.semaphore_signal(barrier, inc=1, device_id=device, device_id_type=MESH)
    pl.semaphore_wait(barrier, len(devices))


class GatherHidden:
    def __init__(self, me, links, view):
        self.me, self.links, self.view = me, links, view

    def start(self):
        own = self.view(self.me.h)
        self.by_side = self.links.copy(own, own, self.me.side)
        self.by_core = self.links.copy(own, own, self.me.core)

    def forward(self):
        self.by_side.wait_recv()
        far = self.view(self.me.hx)
        self.by_far = self.links.copy(far, far, self.me.core)


class GatherBatch:
    def __init__(self, me, links, view):
        self.me, self.links, self.view = me, links, view

    def start(self):
        ends = ((0, self.me.ydev), (1, self.me.zdev), (1, self.me.ydev), (0, self.me.zdev))
        own = [self.view(self.me.p, 0), self.view(self.me.p, 1)]
        self.y0, self.z1, self.y1, self.z0 = (self.links.copy(own[n], own[n], device) for n, device in ends)

    def forward(self):
        self.y0.wait_recv()
        part = self.view(self.me.py, 0)
        self.on_z = self.links.copy(part, part, self.me.zdev)
        self.z1.wait_recv()
        part = self.view(self.me.pz, 1)
        self.on_y = self.links.copy(part, part, self.me.ydev)

    def arrive(self):
        self.y1.wait_recv()
        self.z0.wait_recv()

    def finish(self):
        self.on_z.wait_recv()
        self.on_y.wait_recv()

    def sent(self):
        return [self.y0, self.y1, self.z0, self.z1, self.on_y, self.on_z]


class Scatter:
    def __init__(self, me, links, rows, sc, rc, sx, rx, acc):
        self.me, self.links, self.rows, self.sent = me, links, rows, []
        self.sc, self.rc, self.sx, self.rx, self.acc = sc, rc, sx, rx, acc

    def run(self, prepare, block, hook):
        x, c, cut = self.me.x, self.me.c, pl.ds(0, self.rows)
        for n, start in enumerate((2 * (1 - x), 2 * x)):
            away, home = start + 1 - c, start + c

            def send(i, value):
                self.sc[n, i, cut] = value.astype(LOW)

            def keep(i, value):
                value = value + self.rc[n, i, cut].astype(F32)
                if n == 0:
                    self.sx[i] = value.astype(LOW)
                else:
                    self.acc[i, cut] = value

            prepare(0, away)
            block(0, away, send)
            by_core = self.links.copy(self.sc.at[n, :, cut], self.rc.at[n, :, cut], self.me.core)
            self.sent.append(by_core)
            prepare(1, home)
            by_core.wait_recv()
            block(1, home, keep)
            if n == 0:
                self.by_side = self.links.copy(self.sx, self.rx, self.me.side)
                self.sent.append(self.by_side)
                hook()

    def wait(self):
        self.by_side.wait_recv()

    def value(self, i):
        return self.acc[i, 0 : self.rows] + self.rx[i].astype(F32)


class Share:
    def __init__(self, me, links, rows, sc, rc, acc):
        self.me, self.links, self.cut = me, links, pl.ds(0, rows)
        self.sc, self.rc, self.acc = sc, rc, acc

    def away(self, block):
        def sink(i, value):
            self.sc[i, self.cut] = value.astype(LOW)

        block(1 - self.me.c, sink)
        self.by_core = self.links.copy(self.sc.at[:, self.cut], self.rc.at[:, self.cut], self.me.core)

    def home(self, block):
        def sink(i, value):
            self.acc[i, self.cut] = value

        block(self.me.c, sink)

    def wait(self):
        self.by_core.wait_recv()

    def value(self, i):
        return self.acc[i, self.cut] + self.rc[i, self.cut].astype(F32)


class Reduce:
    def __init__(self, me, links, order, given, given_landing, total, low, landing, whole):
        self.me, self.links, self.order = me, links, order
        self.given, self.given_landing = given, given_landing
        self.total, self.low, self.landing, self.whole = total, low, landing, whole
        self.blocks = total.shape[1] // whole.shape[2]
        bits, size = len(me.bit), total.shape[0]
        kinds = {"x": self.cross, "y": self.halve, "z": self.quarter}
        self.plan = [(kinds[axis], 0) for axis in order]
        more = extra_halvings(size, bits)
        self.plan += [(self.halve, k) for k in range(3, 3 + more)]
        self.plan += [(self.double, k) for k in range(3 + more, bits)]
        back = [(self.gather_half, k) for k in reversed(range(3, 3 + more))]
        back += [({"y": self.gather_half, "z": self.gather_quarters}[axis], 0) for axis in reversed(order) if axis != "x"]
        self.plan += back
        self.first_back = len(self.plan) - len(back)
        self.doubled = bits > 3 + more
        self.at, self.used, self.spans, self.crossed, self.after = 0, 0, [(0, size)], False, None

    def span(self, first, size):
        return pl.ds(pl.multiple_of(first, 16), size)

    def end(self):
        if self.after is not None:
            self.after()
            self.after = None

    def step(self):
        self.end()
        if self.at == len(self.plan):
            return False
        if self.at == self.first_back:
            mine, wide = self.span(*self.spans[-1]), self.whole.shape[2]
            own = self.low if self.doubled else self.total
            for n in range(self.blocks):
                self.whole[n, mine, :] = own[mine, n * wide : (n + 1) * wide].astype(LOW)
        kind, k = self.plan[self.at]
        self.at += 1
        kind(k)
        return True

    def land(self, size):
        self.used += size
        return pl.ds(self.used - size, size)

    def add(self, made, mine, place):
        made.wait_recv()
        self.add_rows(mine, self.landing, place.start)

    def add_rows(self, mine, landing, start):
        def some(at, i, step):
            self.total[pl.ds(at, step), :] += landing[pl.ds(start + i, step), :].astype(F32)

        by_rows(mine.start, mine.size, some)

    def send(self, first, size, device):
        give, place = self.span(first, size), self.land(size)

        def some(at, i, step):
            self.low[pl.ds(at, step), :] = self.total[pl.ds(at, step), :].astype(LOW)

        by_rows(first, size, some)
        return self.links.copy(self.low.at[give], self.landing.at[place], device), place

    def cross(self, _):
        first, size = self.spans[-1]
        mine, place = self.span(first, size), pl.ds(self.given.shape[0] - size, size)
        made = self.links.copy(self.given.at[mine], self.given_landing.at[place], self.me.side)
        self.crossed = True

        def after():
            made.wait_recv()
            self.add_rows(mine, self.given_landing, place.start)

        self.after = after

    def halve(self, k):
        first, size = self.spans[-1]
        half, u = size // 2, self.me.bit[k]
        keep, away = first + u * half, first + (1 - u) * half
        mine = self.span(keep, half)
        self.spans.append((keep, half))
        far = None
        if not self.crossed:
            far = self.links.copy(self.given.at[self.span(away, half)], self.given_landing.at[pl.ds(0, half)], self.me.flip[k])
        made, place = self.send(away, half, self.me.flip[k])

        def after():
            if far is not None:
                far.wait_recv()

                def some(at, i, step):
                    rows = pl.ds(at, step)
                    total = self.given[rows, :].astype(F32) + self.given_landing[pl.ds(i, step), :].astype(F32)
                    self.given[rows, :] = total.astype(LOW)

                by_rows(keep, half, some)
            self.add(made, mine, place)

        self.after = after

    def column(self, d):
        v = self.me.bit[1] + 2 * self.me.bit[2]
        w = lax.rem(v + d, 4)
        return w, {"batch": self.me.b + 2 * (w - v)}

    def quarter(self, _):
        first, size = self.spans[-1]
        part = size // 4
        keep = first + (self.me.bit[1] + 2 * self.me.bit[2]) * part
        self.spans.append((keep, part))
        made = []
        for d in (2, 1, 3):
            w, device = self.column(d)
            made.append(self.send(first + w * part, part, device))

        def after():
            for one, place in made:
                self.add(one, self.span(keep, part), place)

        self.after = after

    def double(self, k):
        mine = self.span(*self.spans[-1])
        place = self.land(self.spans[-1][1])
        if self.plan[self.at - 2][0] != self.double:
            self.low[mine, :] = self.total[mine, :].astype(LOW)
        made = self.links.copy(self.low.at[mine], self.landing.at[place], self.me.flip[k])

        def after():
            made.wait_recv()
            self.links.settle([made])
            self.low[mine, :] = (self.low[mine, :].astype(F32) + self.landing[place, :].astype(F32)).astype(LOW)

        self.after = after

    def gather(self, devices):
        part = self.whole.at[pl.ds(0, self.blocks), self.span(*self.spans.pop())]
        made = [self.links.copy(part, part, device) for device in devices]

        def after():
            for one in made:
                one.wait_recv()

        self.after = after

    def gather_half(self, k):
        self.gather([self.me.flip[k]])

    def gather_quarters(self, _):
        self.gather([self.column(d)[1] for d in (2, 1, 3)])


def extra_halvings(size, bits):
    count, left = 0, size // 8
    while 3 + count < bits and (left // 2) % 16 == 0:
        count, left = count + 1, left // 2
    return count


def landing_rows(size, bits):
    more, left = extra_halvings(size, bits), size // 8
    return 7 * left + sum(left >> (k + 1) for k in range(more)) + (bits - 3 - more) * (left >> more)


def chunk_rows(units):
    third = units // 3
    return (third,) * 3, (third,) * 3


def columns(t, size):
    return pl.ds(pl.multiple_of(t * size, size), size)


def loop(count, body):
    def one(i, carry):
        body(i)
        return carry

    lax.fori_loop(0, count, one, 0)


def by_rows(first, size, body):
    step = min(size, 32)

    def one(i):
        body(pl.multiple_of(first + i * step, 16), pl.multiple_of(i * step, 16), step)

    loop(size // step, one)


ROOT = math.sqrt(2 / math.pi)
CUBE = 0.044715


def gelu_both(v):
    square = v * v
    t = jnp.tanh(v * (ROOT + ROOT * CUBE * square))
    half = 0.5 + 0.5 * t
    slope = half + (0.5 * v) * (1 - t * t) * (ROOT + 3 * ROOT * CUBE * square)
    return v * half, slope


def up(value):
    return jnp.sum(value, 0, keepdims=True)


SCHEDULE = (
    ("keep", 0), ("give", 0), ("chunk", 1), ("chunk", 0), ("back", 0), ("norm", 0), ("back", 1), ("chunk", 1),
    ("give", 1), ("chunk", 4), ("chunk", 3), ("near", 0), ("far", 0), ("halves", 0), ("chunk", 0), ("chunk", 2),
    ("chunk", 1), ("keep", 1), ("chunk", 4), ("chunk", 3), ("chunk", 5), ("chunk", 1), ("norm", 1), ("pack", 0),
    ("chunk", 0), ("chunk", 2), ("chunk", 3), ("chunk", 0), ("ends", 0), ("near", 1), ("chunk", 4), ("far", 1),
    ("chunk", 1), ("chunk", 3), ("chunk", 2), ("chunk", 5), ("chunk", 5), ("chunk", 4), ("sequence", 0), ("order", 0),
    ("small", 0), ("chunk", 3), ("round", 0), ("chunk", 2), ("grad", 0), ("ends", 1), ("halves", 1), ("chunk", 0),
    ("chunk", 5), ("chunk", 4), ("chunk", 2), ("sequence", 1), ("order", 1), ("chunk", 5), ("chunk", 1), ("round", 0),
    ("chunk", 4), ("grad", 1), ("chunk", 3), ("chunk", 2), ("chunk", 0), ("chunk", 5),
)
ORDERS = ("yxz", "yxz", "yxz", "xyz", "xzy", "yxz")


def layer_kernel(
    bits,
    x_hbm, cot_hbm, w1_hbm, w2_hbm, small_hbm, ht_hbm, gt_hbm, order_hbm,
    g1_ref, s1_ref, bo_ref, g2_ref, s2_ref, bin_ref, live_ref,
    out_hbm, grad_hbm, wg1_hbm, wg2_hbm, light_ref, bias_ref,
    tab, small, ht, gt, order, xg, cs, ct, og, ab, sc, rc, sx, rx, acc, yf, hf, df, zf, u1, gr2, inv1, lanes,
    wr, wt, wg, given, landing, ug, rowv, rows_in, pn, lsend, lrecv, lbias, ltot, lnext, send, recv, near,
):
    slots, _, piece = x_hbm.shape
    parts, rows, tokens = cs.shape[1:]
    width = parts * rows
    units = wg.shape[1]
    pad = gt.shape[0]
    me = Place(bits)
    links = Links(send, recv, near)
    is_cos = me.c == 0

    def fetch_tokens(src, dst, s):
        return [links.fetch(src.at[s, :, pl.ds(t * tokens, tokens)], dst.at[s, t]) for t in range(parts)]

    x_in = [fetch_tokens(x_hbm, u1, s) for s in range(slots)]
    w1_in, w2_in = links.fetch(w1_hbm, wg.at[0]), links.fetch(w2_hbm, wg.at[1])
    small_in = links.fetch(small_hbm.at[me.p], small)
    cot_in = [fetch_tokens(cot_hbm, gr2, s) for s in range(slots)]
    ht_in = links.fetch(ht_hbm.at[me.h], ht)
    gt_in = links.fetch(gt_hbm.at[me.h], gt)
    order_in = links.fetch(order_hbm.at[me.h], order)
    greet([me.core, me.side, me.cross] + me.flip)

    def input_view(s):
        def view(q, half=None):
            return xg.at[s, q, slice(None) if half is None else pl.ds(half * 2, 2), me.c]

        return view

    spread = [GatherBatch(me, links, input_view(s)) for s in range(slots)]
    over = [[] for _ in range(slots)]

    def hand_over(s, q):
        block = input_view(s)(q)
        over[s].append(links.copy(block, block, me.core))

    for s in range(slots):
        for t in range(parts):
            x_in[s][t].wait()
            xg[s, me.p, t, me.c] = u1[s, t].astype(LOW)
        if s == 0:
            spread[0].start()
        hand_over(s, me.p)

    far = 1 - me.x
    quarter, straight = units // SPLIT, width - 128

    def weight_view(q, half=None):
        at = pl.ds(pl.multiple_of(q * quarter, 16), quarter)
        return wr.at[slice(None) if half is None else pl.ds(half, 1), far, at, pl.ds(0, straight)]

    weights = GatherBatch(me, links, weight_view)
    w1_in.wait()
    w2_in.wait()

    def own_weights(r, carry):
        at = columns(r, 256)
        for n in range(units // 256):
            cut = slice(n * 256, (n + 1) * 256)
            first, second = wg[0, at, cut], wg[1, at, cut]
            wt[0, me.x, at, cut] = first.astype(LOW)
            wr[0, me.x, cut, at] = first.T.astype(LOW)
            wr[1, me.x, at, cut] = second.astype(LOW)
            wt[1, me.x, cut, at] = second.T.astype(LOW)
        return carry

    lax.fori_loop(0, units // 256, own_weights, 0)
    quarter_at = pl.ds(pl.multiple_of(me.p * quarter, 16), quarter)
    mine_w = wr.at[:, me.x, quarter_at, pl.ds(0, straight)]
    by_side = links.copy(mine_w, mine_w, me.side)
    mine_w = wr.at[:, me.x, :, pl.ds(straight, 128)]
    direct = links.copy(mine_w, mine_w, me.side)

    vectors = (g1_ref, s1_ref, bo_ref, g2_ref, s2_ref)
    rowv[...] = jnp.zeros_like(rowv)
    for k, ref in enumerate(vectors):
        rowv[k : k + 1, 0:rows] = ref[...]
    for i in range(parts):
        rowv[5 + i : 6 + i, 0:rows] = bin_ref[:, i * rows : (i + 1) * rows]
    params = [links.copy(rowv, rows_in.at[me.h], device) for device in (me.core, me.side, me.cross)]

    small_in.wait()

    def make_rows(i, carry):
        big_cos, big_sin = small[0, pl.ds(i, 1), :], small[1, pl.ds(i, 1), :]
        by_cos = jnp.where(is_cos, big_cos, big_sin)
        by_sin = jnp.where(is_cos, -big_sin, big_cos)
        at = pl.ds(pl.multiple_of(i * FINE, FINE), FINE)
        for n in range(piece // 256):
            cut = slice(n * 256, (n + 1) * 256)
            tab[at, cut] = (by_cos[:, cut] * small[2, :, cut] + by_sin[:, cut] * small[3, :, cut]).astype(LOW)
        return carry

    lax.fori_loop(0, FINE, make_rows, 0)
    spread[0].forward()
    spread[1].start()
    for s in range(slots):
        for t in range(parts):
            cot_in[s][t].wait()
            cs[s, t] = (gr2[s, t] * live_ref[s]).astype(LOW)
        ct[s, me.h] = cs[s, me.h]
    ht_in.wait()

    sums = [
        Scatter(me, links, rows, sc.at[s], rc.at[s], sx.at[s], rx.at[s], acc.at[s]) for s in range(slots)
    ]

    def prepare(s, j, t):
        at = columns(t, tokens)
        total = None
        for q in range(SPLIT):
            for n in range(parts):
                first = q * piece + n * tokens
                share = dot(xg[s, q, n].reshape(2 * rows, tokens), tab[first : first + tokens, at])
                total = share if total is None else total + share
        ab[j] = total.astype(LOW)

    def transform(s, j, t, sink):
        def one(i):
            own = jnp.where(me.h == i, 1.0, 0.0).astype(F32)
            sink(i, dot(ht[i], ab[j]) + own * u1[s, t])

        loop(parts, one)

    moved = []

    def next_input():
        spread[1].forward()
        by_side.wait_recv()
        weights.start()

    def next_weights():
        weights.forward()

    for s, hook in enumerate((next_input, next_weights)):
        spread[s].arrive()
        hand_over(s, me.py)
        hand_over(s, me.pz)
        spread[s].finish()
        hand_over(s, me.pd)
        for made in over[s]:
            made.wait_recv()
        sums[s].run(functools.partial(prepare, s), functools.partial(transform, s), hook)
        for to, device in ((me.hc, me.core), (me.hx, me.side), (me.hd, me.cross)):
            moved.append(links.copy(cs.at[s, to], ct.at[s, me.h], device))
        links.settle(over[s] + spread[s].sent())
    for made in params:
        made.wait_recv()
    rows_in[me.h] = rowv[...]
    square = jnp.zeros((128 - rowv.shape[0], rowv.shape[1]), F32)
    for i in range(parts):
        pn[i] = jnp.concatenate([rows_in[i], square], 0).T[0:rows, :]

    def param(k, i):
        return pn[i, :, k : k + 1]

    def folded(value):
        return value[:, :128] + value[:, 128:]

    def lane_sum(k, i, s, value):
        lanes[k, i] = folded(value) if s == 0 else lanes[k, i] + folded(value)

    def row_sums(body):
        sums_of = [[up(value) for value in body(i)] for i in range(parts)]
        return [functools.reduce(jnp.add, values) for values in zip(*sums_of)]

    def each(body):
        for i in range(parts):
            body(i)

    def mean_and_inverse(total, squares):
        mean = total / width
        return mean, lax.rsqrt(squares / width - mean * mean + EPS)

    def part_rows(i):
        return pl.ds(i * rows, rows)

    def norm_first(s):
        whole = sums[s].acc

        def resid(i):
            v = sums[s].value(i)
            whole[i, 0:rows] = v
            return v, v * v

        mean, inverse = mean_and_inverse(*row_sums(resid))
        inv1[s] = inverse

        def one(i):
            u = (whole[i, 0:rows] - mean) * inverse
            u1[s, i] = u
            yf[s, me.c, part_rows(i), :] = (u * param(0, i) + param(1, i)).astype(LOW)

        each(one)

    def forward_in(s, k, unit):
        def one(i):
            at = part_rows(i)
            h, slope = gelu_both(dot(wr[0, unit, at, :], yf[s, k]) + pn[2 * unit + me.c, :, 5 + i : 6 + i])
            hf[s, 2 * k + unit, at, :] = h.astype(LOW)
            df[s, 2 * k + unit, at, :] = slope.astype(LOW)

        each(one)

    def forward_out(s, k, sink):
        def one(i):
            at = part_rows(i)
            sink(i, dot(wt[1, 0, at, :], hf[s, 2 * k]) + dot(wt[1, 1, at, :], hf[s, 2 * k + 1]))

        each(one)

    def norm_second(s, shared):
        whole = shared.acc

        def resid(i):
            v = u1[s, i] * param(0, i) + param(1, i) + shared.value(i) + param(2, i)
            whole[i, 0:rows] = v
            return v, v * v

        mean, inverse = mean_and_inverse(*row_sums(resid))

        def unit(i):
            u = (whole[i, 0:rows] - mean) * inverse
            whole[i, 0:rows] = u
            cs[s, i] = (u * param(3, i) + param(4, i)).astype(LOW)
            g = ct[s, i].astype(F32)
            lane_sum(0, i, s, g * u)
            lane_sum(1, i, s, g)
            q = g * param(3, i)
            return q, q * u

        total, cross = row_sums(unit)
        total, cross = total / width, cross / width

        def one(i):
            q = ct[s, i].astype(F32) * param(3, i)
            grad = inverse * (q - total - whole[i, 0:rows] * cross)
            gr2[s, i] = grad
            lane_sum(2, i, s, grad)
            zf[s, me.c, part_rows(i), :] = grad.astype(LOW)

        each(one)

    def backward_in(s, k, fresh):
        for unit in range(2):

            def one(i):
                at = part_rows(i)
                gp = dot(wr[1, unit, at, :], zf[s, k]) * df[s, 2 * k + unit, at, :].astype(F32)
                place = 5 + unit
                lanes[place, i] = folded(gp) if fresh else lanes[place, i] + folded(gp)
                df[s, 2 * k + unit, at, :] = gp.astype(LOW)

            each(one)

    def backward_out(s, k, sink):
        def one(i):
            at = part_rows(i)
            sink(i, dot(wt[0, 0, at, :], df[s, 2 * k]) + dot(wt[0, 1, at, :], df[s, 2 * k + 1]))

        each(one)

    def weight_grad(which, unit, store):
        def one(r, carry):
            at = columns(r, 256)
            for n in range(units // 256):
                cut = slice(n * 256, (n + 1) * 256)
                total = 0.0
                for s in range(slots):
                    for k in range(2):
                        if which == 0:
                            total = total + dot_rows(hf[s, 2 * k + unit, at, :], zf[s, k, cut, :])
                        else:
                            total = total + dot_rows(yf[s, k, at, :], df[s, 2 * k + unit, cut, :])
                store(which, at, cut, total)
            return carry

        lax.fori_loop(0, units // 256, one, 0)

    def norm_first_back(s, shared):
        whole = shared.acc

        def entry(i):
            grad = gr2[s, i] + shared.value(i)
            whole[i, 0:rows] = grad
            u = u1[s, i]
            lane_sum(3, i, s, grad * u)
            lane_sum(4, i, s, grad)
            q = grad * param(0, i)
            return q, q * u

        total, cross = row_sums(entry)
        total, cross = total / width, cross / width

        def one(i):
            q = whole[i, 0:rows] * param(0, i)
            xg[s, me.h, i, 0] = (inv1[s] * (q - total - u1[s, i] * cross)).astype(LOW)

        each(one)

    def to_core(block):
        return links.copy(block, block, me.core)

    outward = [Share(me, links, rows, sc.at[s, 0], rc.at[s, 0], acc.at[s]) for s in range(slots)]
    inward = [Share(me, links, rows, sc.at[s, 1], rc.at[s, 1], acc.at[s]) for s in range(slots)]

    def enter(s):
        sums[s].wait()
        norm_first(s)
        got = to_core(yf.at[s, me.c])
        forward_in(s, me.c, me.x)
        got.wait_recv()
        forward_in(s, 1 - me.c, me.x)

    def leave(s):
        links.settle(sums[s].sent)
        forward_in(s, 1 - me.c, far)
        forward_in(s, me.c, far)
        outward[s].away(functools.partial(forward_out, s))
        outward[s].home(functools.partial(forward_out, s))

    def far_weights(r, carry):
        at = columns(r, 256)
        for n in range(units // 256):
            cut = slice(n * 256, (n + 1) * 256)
            wt[0, far, cut, at] = wr[0, far, at, cut].astype(F32).T.astype(LOW)
            wt[1, far, cut, at] = wr[1, far, at, cut].astype(F32).T.astype(LOW)
        return carry

    enter(0)
    weights.arrive()
    weights.finish()
    direct.wait_recv()
    lax.fori_loop(0, units // 256, far_weights, 0)
    links.settle([by_side, direct] + weights.sent())
    leave(0)
    enter(1)
    leave(1)
    for made in moved:
        made.wait_recv()
    links.settle(moved)
    seconds, outs = [], {}
    for s in range(slots):
        outward[s].wait()
        norm_second(s, outward[s])
        seconds.append(to_core(zf.at[s, me.c]))
        og[s, me.h] = cs[s, me.h]
        outs[s] = [
            links.copy(cs.at[s, to], og.at[s, me.h], device)
            for to, device in ((me.hc, me.core), (me.hx, me.side), (me.hd, me.cross))
        ]

    def mix_view(s):
        return lambda t: xg.at[s, t, :, 0]

    def freq_view(s):
        cuts = (pl.ds(0, pad // 32 * 16), pl.ds(pad // 32 * 16, pad - pad // 32 * 16))

        def view(q, half=None):
            return ug.at[s, q] if half is None else ug.at[s, q, cuts[half]]

        return view

    gathers = [GatherHidden(me, links, mix_view(s)) for s in range(slots)]
    spreads = [GatherBatch(me, links, freq_view(s)) for s in range(slots)]
    heavy, chunks = [], []
    for which, whole in ((0, hf), (1, df)):
        low, used = 0, 0
        for size in chunk_rows(units)[which]:
            at, place = pl.ds(low, size), pl.ds(used, landing_rows(size, bits))
            low, used = low + size, used + landing_rows(size, bits)
            chunks.append((which, at))
            heavy.append(
                Reduce(
                    me, links, ORDERS[len(heavy)], wr.at[0, which, at], given.at[which, at], wg.at[which, at], wt.at[1, which, at],
                    landing.at[which, place], whole.at[0, :, at],
                )
            )

    def features(s, t):
        whole = jnp.concatenate([xg[s, t, i, 0] for i in range(parts)], 0)
        ug[s, me.p, :, columns(t, tokens)] = dot(gt[...], whole).astype(LOW)

    def store_given(which, at, cut, value):
        wr[0, which, at, cut] = value.astype(LOW)

    def store_kept(which, at, cut, value):
        wg[which, at, cut] = value

    for made in seconds:
        made.wait_recv()

    def backward(s):
        backward_in(s, me.c, s == 0)
        backward_in(s, 1 - me.c, False)
        inward[s].away(functools.partial(backward_out, s))
        inward[s].home(functools.partial(backward_out, s))

    def first_back(s):
        inward[s].wait()
        norm_first_back(s, inward[s])
        gathers[s].start()

    def near_features(s):
        features(s, me.h)
        gathers[s].by_core.wait_recv()
        features(s, me.hc)

    def far_features(s):
        gathers[s].forward()
        features(s, me.hx)
        gathers[s].by_far.wait_recv()
        features(s, me.hd)
        spreads[s].start()

    ones = jnp.ones((8, 128), F32)

    def lane_total(k, i):
        return lax.dot_general(
            ones, lanes[k, i], (((1,), (1,)), ((), ())), precision=lax.Precision.HIGHEST, preferred_element_type=F32
        )

    row = lax.broadcasted_iota(jnp.int32, (8, rows), 0)
    light = []

    def start_small_sums():
        for i in range(parts):
            packed = jnp.zeros((8, rows), F32)
            for k in range(5):
                packed = jnp.where(row == k, lane_total(k, i), packed)
            lsend[i] = packed
        for unit in range(2):
            packed = jnp.zeros((8, rows), F32)
            for i in range(parts):
                packed = jnp.where(row == i, lane_total(5 + unit, i), packed)
            lbias[unit] = packed
        for to, device in ((me.hc, me.core), (me.hx, me.side), (me.hd, me.cross)):
            light.append(links.copy(lsend.at[to], lrecv.at[me.h], device))
        light.append(links.copy(lbias.at[far], lbias.at[2], me.side))

    sign = jnp.where((me.h == 0) | (me.h == 3), -1.0, 1.0).astype(F32)
    mine = jnp.where(is_cos, 1.0, sign)
    theirs = jnp.where(is_cos, sign, 1.0)
    stored = []

    def sequence(s):
        spreads[s].arrive()
        spreads[s].finish()
        links.settle([outward[s].by_core])

        def one(t):
            at = columns(t, tokens)
            total = None
            for q in range(SPLIT):
                share = dot(ug[s, q], tab[q * piece : (q + 1) * piece, at])
                total = share if total is None else total + share
            acc[s, t] = total
            sc[s, 0, t] = total.astype(LOW)

        loop(parts, one)
        swaps[s] = links.copy(sc.at[s, 0], rc.at[s, 0], me.core)

    swaps, across = {}, {}

    def ordered(s):
        swaps[s].wait_recv()

        def one(t):
            pair = (mine * acc[s, t] + theirs * rc[s, 0, t].astype(F32)).astype(LOW)
            sx[s, t] = dot(order[...], pair).astype(LOW)

        loop(parts, one)
        made = links.describe(sx.at[s], rx.at[s], me.side)
        across[s] = made

        @pl.when(jnp.logical_not(is_cos))
        def _():
            made.start()

    def store_grad(s):
        def store(part):
            def one(t):
                u1[s, t] = part[s, t].astype(F32) + xg[s, t, me.h, 0].astype(F32)

            loop(parts, one)

        @pl.when(is_cos)
        def _():
            store(sx)

        @pl.when(jnp.logical_not(is_cos))
        def _():
            across[s].wait()
            store(rx)

        for t in range(parts):
            stored.append(links.fetch(u1.at[s, t], grad_hbm.at[s, :, pl.ds(t * tokens, tokens)]))

    def end_outs(s):
        for made in outs[s]:
            made.wait_recv()
        for t in range(parts):
            gr2[s, t] = og[s, t].astype(F32) * live_ref[s]
            stored.append(links.fetch(gr2.at[s, t], out_hbm.at[s, :, pl.ds(t * tokens, tokens)]))

    def small_sums():
        for made in light:
            made.wait_recv()
        ltot[0, 0:8] = lsend[me.h] + lrecv[me.hc] + lrecv[me.hx] + lrecv[me.hd]
        ltot[0, 8:16] = lbias[me.x] + lbias[2]
        small_round()

    rounds = []

    def small_round():
        k = len(rounds)
        if k:
            rounds[k - 1].wait_recv()
            ltot[k] = ltot[k - 1] + lnext[k - 1]
        if k < bits:
            rounds.append(links.copy(ltot.at[k], lnext.at[k], me.flip[k]))

    def store_chunk(n):
        which, at = chunks[n]
        dst = (wg2_hbm, wg1_hbm)[which].at[at]
        for m in range(heavy[n].blocks):
            stored.append(links.fetch(heavy[n].whole.at[m], dst.at[:, pl.ds(m * tokens, tokens)]))

    def step(n):
        if not heavy[n].step():
            store_chunk(n)
            return False
        return True

    acts = {
        "back": backward,
        "norm": first_back,
        "near": near_features,
        "far": far_features,
        "halves": lambda s: spreads[s].forward(),
        "sequence": sequence,
        "order": ordered,
        "grad": store_grad,
        "give": lambda which: weight_grad(which, far, store_given),
        "keep": lambda which: weight_grad(which, me.x, store_kept),
        "pack": lambda _: start_small_sums(),
        "small": lambda _: small_sums(),
        "round": lambda _: small_round(),
        "ends": end_outs,
        "chunk": lambda n: step(n),
    }
    going = [True] * len(heavy)
    gt_in.wait()
    order_in.wait()
    for kind, n in SCHEDULE:
        did = acts[kind](n)
        if kind == "chunk":
            going[n] = did
    while any(going):
        for n in range(len(heavy)):
            going[n] = going[n] and step(n)
        if len(rounds) < bits:
            small_round()
    while len(rounds) < bits:
        small_round()
    k = bits - 1
    if len(rounds) == bits:
        rounds[k].wait_recv()
        ltot[bits] = ltot[k] + lnext[k]
    light_ref[...] = ltot[bits, 0:8]
    for i in range(parts):
        bias_ref[:, i * rows : (i + 1) * rows] = ltot[bits, 8 + i : 9 + i]
    for made in stored:
        made.wait()
    for made in list(links.open):
        made.wait_send()


def local(
    n_batch,
    layer_input,
    gain_first,
    shift_first,
    weight_in,
    bias_in,
    weight_out,
    bias_out,
    gain_second,
    shift_second,
    cotangent,
    live_counts,
):
    slots, rows, piece = layer_input.shape
    width = rows * HOLD
    tokens = piece // HOLD
    units = weight_in.shape[1]
    length = piece * SPLIT
    pad = rows + 16
    bits = n_batch.bit_length() - 1
    live = (jnp.arange(slots) < live_counts[0]).astype(F32)
    vectors = (gain_first, shift_first, bias_out, gain_second, shift_second, bias_in)
    small = sequence_tables(length, SPLIT)
    forward, backward, order = feature_tables(width, HOLD)
    any_, vmem = pl.BlockSpec(memory_space=pl.ANY), pl.BlockSpec(memory_space=pltpu.VMEM)
    block = (HOLD, rows, tokens)
    padded = (HOLD, pad, tokens)
    shard = (slots,) + block
    landing = max(sum(landing_rows(size, bits) for size in sizes) for sizes in chunk_rows(units))
    scratch = [
        ((length, piece), LOW), ((4, FINE, piece), F32), (forward.shape[1:], LOW), (backward.shape[1:], LOW),
        (order.shape[1:], LOW), ((slots, SPLIT, HOLD, 2, rows, tokens), LOW), (shard, LOW), (shard, LOW), (shard, LOW),
        ((2, 2 * rows, tokens), LOW), ((slots, 2) + padded, LOW), ((slots, 2) + padded, LOW), (shard, LOW), (shard, LOW),
        ((slots,) + padded, F32), ((slots, 2, width, tokens), LOW), ((slots, 4, units, tokens), LOW),
        ((slots, 4, units, tokens), LOW), ((slots, 2, width, tokens), LOW), (shard, F32), (shard, F32),
        ((slots, 1, tokens), F32), ((7, HOLD, rows, 128), F32),
        ((2, 2, units, width), LOW), ((2, 2, width, units), LOW), ((2, units, width), F32),
        ((2, units, width), LOW), ((2, landing, width), LOW),
        ((slots, SPLIT, pad, piece), LOW), ((16, 256), F32), ((HOLD, 16, 256), F32), ((HOLD, rows, 128), F32), ((HOLD, 8, rows), F32),
        ((HOLD, 8, rows), F32), ((3, 8, rows), F32), ((bits + 1, 16, rows), F32), ((bits, 16, rows), F32),
    ]
    outs = [
        (layer_input.shape, F32), (layer_input.shape, F32), ((width, units), LOW), ((units, width), LOW),
        ((8, rows), F32), ((1, units), F32),
    ]
    out, grad, wg1, wg2, light, bias = pl.pallas_call(
        functools.partial(layer_kernel, bits),
        name="layer",
        out_shape=[jax.ShapeDtypeStruct(shape, kind) for shape, kind in outs],
        in_specs=[any_] * 8 + [vmem] * 6 + [pl.BlockSpec(memory_space=pltpu.SMEM)],
        out_specs=[any_] * 4 + [vmem] * 2,
        scratch_shapes=[pltpu.VMEM(shape, kind) for shape, kind in scratch]
        + [pltpu.SemaphoreType.DMA((192,)), pltpu.SemaphoreType.DMA((192,)), pltpu.SemaphoreType.DMA((96,))],
        compiler_params=pltpu.CompilerParams(
            collective_id=1, has_side_effects=True, vmem_limit_bytes=VMEM_LIMIT
        ),
    )(
        layer_input, cotangent, weight_in, weight_out, jnp.asarray(small), jnp.asarray(forward),
        jnp.asarray(backward), jnp.asarray(order), *(v.reshape(1, -1) for v in vectors), live,
    )
    return (
        out, grad, light[3], light[4], wg1.astype(F32), bias.reshape(units), wg2.astype(F32),
        light[2], light[0], light[1],
    )


def solution(mesh):
    return jax.shard_map(
        functools.partial(local, mesh.shape["batch"]),
        mesh=mesh,
        in_specs=(
            P(None, "hidden", "batch"),
            P("hidden"),
            P("hidden"),
            P(None, "hidden"),
            P("hidden"),
            P("hidden", None),
            P("hidden"),
            P("hidden"),
            P("hidden"),
            P(None, "hidden", "batch"),
            P("batch"),
        ),
        out_specs=(
            P(None, "hidden", "batch"),
            P(None, "hidden", "batch"),
            P("hidden"),
            P("hidden"),
            P(None, "hidden"),
            P("hidden"),
            P("hidden", None),
            P("hidden"),
            P("hidden"),
            P("hidden"),
        ),
        check_vma=False,
    )
```

profile of v0, /device:TPU:0, one launch (start us, length us, event | category | flops | bytes accessed | tf_op | source)
XLA Modules:
  0.0 182.6 jit_solution(15607572308685361685)
XLA Ops:
  1.3 0.5 compare_convert_fusion.live_ref
  1.8 1.3 reshape.46.bin_ref
  3.1 168.6 %layer.1 = (f32[2,192,1024]{2,1,0:T(8,128)}, f32[2,192,1024]{2,1,0:T(8,128)}, bf16[768,768]{1,0:T(8,128)(2,1)}, bf16[768,768]{1,0:T(8,128)(2,1)}, f32[8,192]{1,0:T(8,128)}, /*index=5*/f32[1,768]{1,0:T(1,128)}) custom-call(f32[2,192,1024]{2,1,0:T(8,128)} %x_hbm.1, f32[2,192,1024]{2,1,0:T(8,128)} %cot_hbm.1, f32[768,768]{1,0:T(8,128)} %w1_hbm.1, ...), custom_call_target="tpu_custom_call" | custom-call | tf_op jit(solution)/shard_map/layer/pallas_call | solution.py:1090
  171.7 1.3 reduce
  173.0 1.5 fusion
  174.4 0.0 copy-start.2
  174.4 2.9 %convert_element_type.10 = f32[768,768]{1,0:T(8,128)} convert(bf16[768,768]{1,0:T(8,128)(2,1)} %get-tuple-element.19) | non-fusion elementwise | flops 589824 | bytes 3538944 | tf_op jit(solution)/shard_map/convert_element_type | solution.py:1106
  177.4 0.0 copy-done.2
  177.4 0.0 copy-start.1
  177.4 1.6 convert_element_type.11
  178.9 0.5 copy-done.1
  179.5 0.0 copy-start
  179.5 1.1 copy.28
  180.6 0.8 copy-done
  181.5 1.1 copy.29
Async XLA Ops:
  174.4 2.9 %copy-start.2 = (bf16[768,768]{1,0:T(8,128)(2,1)S(1)}, bf16[768,768]{1,0:T(8,128)(2,1)}, u32[]{:S(2)}) copy-start(bf16[768,768]{1,0:T(8,128)(2,1)} %get-tuple-element.21) | copy-start | bytes 3538948
  177.4 2.1 %copy-start.1 = (f32[2,192,1024]{2,1,0:T(8,128)S(1)}, f32[2,192,1024]{2,1,0:T(8,128)}, u32[]{:S(2)}) copy-start(f32[2,192,1024]{2,1,0:T(8,128)} %get-tuple-element.37) | copy-start | bytes 4718596
  179.5 2.0 %copy-start = (f32[2,192,1024]{2,1,0:T(8,128)S(1)}, f32[2,192,1024]{2,1,0:T(8,128)}, u32[]{:S(2)}) copy-start(f32[2,192,1024]{2,1,0:T(8,128)} %get-tuple-element.38) | copy-start | bytes 4718596
where the time goes:
time: 184 us; the launch traced here: 183 us
  Pallas kernels  169 us (92%)
  local copies, waits for them, and re-layouts  6.39 us (3%)
  other arithmetic  6.31 us (3%)
    pallas_call x1, Pallas kernels, local(): pl.pallas_call(functools.partial(layer_kernel, bits), name='layer', out_s...  169 us

commit v1 on v0

--- a/solution.py
+++ b/solution.py
@@ -445,16 +445,16 @@
 
 
 SCHEDULE = (
-    ("keep", 0), ("give", 0), ("chunk", 1), ("chunk", 0), ("back", 0), ("norm", 0), ("back", 1), ("chunk", 1),
-    ("give", 1), ("chunk", 4), ("chunk", 3), ("near", 0), ("far", 0), ("halves", 0), ("chunk", 0), ("chunk", 2),
-    ("chunk", 1), ("keep", 1), ("chunk", 4), ("chunk", 3), ("chunk", 5), ("chunk", 1), ("norm", 1), ("pack", 0),
-    ("chunk", 0), ("chunk", 2), ("chunk", 3), ("chunk", 0), ("ends", 0), ("near", 1), ("chunk", 4), ("far", 1),
-    ("chunk", 1), ("chunk", 3), ("chunk", 2), ("chunk", 5), ("chunk", 5), ("chunk", 4), ("sequence", 0), ("order", 0),
-    ("small", 0), ("chunk", 3), ("round", 0), ("chunk", 2), ("grad", 0), ("ends", 1), ("halves", 1), ("chunk", 0),
-    ("chunk", 5), ("chunk", 4), ("chunk", 2), ("sequence", 1), ("order", 1), ("chunk", 5), ("chunk", 1), ("round", 0),
-    ("chunk", 4), ("grad", 1), ("chunk", 3), ("chunk", 2), ("chunk", 0), ("chunk", 5),
+    ("give", 0), ("chunk", 1), ("keep", 0), ("chunk", 2), ("back", 0), ("back", 1), ("norm", 0), ("give", 1),
+    ("keep", 1), ("chunk", 5), ("chunk", 3), ("chunk", 2), ("chunk", 1), ("near", 0), ("far", 0), ("halves", 0),
+    ("chunk", 3), ("chunk", 5), ("norm", 1), ("chunk", 4), ("chunk", 2), ("pack", 0), ("chunk", 5), ("chunk", 2),
+    ("near", 1), ("chunk", 0), ("chunk", 3), ("chunk", 5), ("far", 1), ("chunk", 4), ("outs", 1), ("chunk", 0),
+    ("chunk", 3), ("small", 0), ("outs", 0), ("sequence", 0), ("order", 0), ("chunk", 2), ("chunk", 4), ("chunk", 1),
+    ("ends", 1), ("chunk", 0), ("halves", 1), ("chunk", 5), ("chunk", 4), ("chunk", 1), ("chunk", 3), ("chunk", 0),
+    ("chunk", 2), ("chunk", 5), ("round", 0), ("chunk", 1), ("ends", 0), ("chunk", 4), ("sequence", 1), ("order", 1),
+    ("chunk", 0), ("grad", 0), ("round", 0), ("chunk", 4), ("chunk", 3), ("grad", 1), ("chunk", 0), ("chunk", 1),
 )
-ORDERS = ("yxz", "yxz", "yxz", "xyz", "xzy", "yxz")
+ORDERS = ("xyz", "xzy", "yxz", "xyz", "yxz", "yxz")
 
 
 def layer_kernel(
@@ -473,6 +473,7 @@
     me = Place(bits)
     links = Links(send, recv, near)
     is_cos = me.c == 0
+    live = [jnp.where(live_ref[0] > s, 1.0, 0.0).astype(F32) for s in range(slots)]
 
     def fetch_tokens(src, dst, s):
         return [links.fetch(src.at[s, :, pl.ds(t * tokens, tokens)], dst.at[s, t]) for t in range(parts)]
@@ -562,7 +563,7 @@
     for s in range(slots):
         for t in range(parts):
             cot_in[s][t].wait()
-            cs[s, t] = (gr2[s, t] * live_ref[s]).astype(LOW)
+            cs[s, t] = (gr2[s, t] * live[s]).astype(LOW)
         ct[s, me.h] = cs[s, me.h]
     ht_in.wait()
 
@@ -809,11 +810,6 @@
         outward[s].wait()
         norm_second(s, outward[s])
         seconds.append(to_core(zf.at[s, me.c]))
-        og[s, me.h] = cs[s, me.h]
-        outs[s] = [
-            links.copy(cs.at[s, to], og.at[s, me.h], device)
-            for to, device in ((me.hc, me.core), (me.hx, me.side), (me.hd, me.cross))
-        ]
 
     def mix_view(s):
         return lambda t: xg.at[s, t, :, 0]
@@ -961,11 +957,18 @@
         for t in range(parts):
             stored.append(links.fetch(u1.at[s, t], grad_hbm.at[s, :, pl.ds(t * tokens, tokens)]))
 
+    def start_outs(s):
+        og[s, me.h] = cs[s, me.h]
+        outs[s] = [
+            links.copy(cs.at[s, to], og.at[s, me.h], device)
+            for to, device in ((me.hc, me.core), (me.hx, me.side), (me.hd, me.cross))
+        ]
+
     def end_outs(s):
         for made in outs[s]:
             made.wait_recv()
         for t in range(parts):
-            gr2[s, t] = og[s, t].astype(F32) * live_ref[s]
+            gr2[s, t] = og[s, t].astype(F32) * live[s]
             stored.append(links.fetch(gr2.at[s, t], out_hbm.at[s, :, pl.ds(t * tokens, tokens)]))
 
     def small_sums():
@@ -1011,6 +1014,7 @@
         "pack": lambda _: start_small_sums(),
         "small": lambda _: small_sums(),
         "round": lambda _: small_round(),
+        "outs": start_outs,
         "ends": end_outs,
         "chunk": lambda n: step(n),
     }
@@ -1062,7 +1066,6 @@
     length = piece * SPLIT
     pad = rows + 16
     bits = n_batch.bit_length() - 1
-    live = (jnp.arange(slots) < live_counts[0]).astype(F32)
     vectors = (gain_first, shift_first, bias_out, gain_second, shift_second, bias_in)
     small = sequence_tables(length, SPLIT)
     forward, backward, order = feature_tables(width, HOLD)
@@ -1100,7 +1103,7 @@
         ),
     )(
         layer_input, cotangent, weight_in, weight_out, jnp.asarray(small), jnp.asarray(forward),
-        jnp.asarray(backward), jnp.asarray(order), *(v.reshape(1, -1) for v in vectors), live,
+        jnp.asarray(backward), jnp.asarray(order), *(v.reshape(1, -1) for v in vectors), live_counts,
     )
     return (
         out, grad, light[3], light[4], wg1.astype(F32), bias.reshape(units), wg2.astype(F32),

time: 184 us -> 174 us (0.946)
  Pallas kernels: 169 us -> 160 us
    pallas_call x1, Pallas kernels: 169 us -> 160 us  [local(): pl.pallas_call(functools.partial(layer_kernel, bits), name='layer', out_s...]
where the time goes in v1:
time: 174 us
  Pallas kernels  160 us (92%)
  local copies, waits for them, and re-layouts  6.39 us (4%)
  other arithmetic  5.8 us (3%)
    pallas_call x1, Pallas kernels, local(): pl.pallas_call(functools.partial(layer_kernel, bits), name='layer', out_s...  160 us
    unnamed x8, local copies, waits for them, and re-layouts  3.66 us

profile of v1, /device:TPU:0, one launch (start us, length us, event | category | flops | bytes accessed | tf_op | source)
XLA Modules:
  0.0 174.0 jit_solution(4896511265287112045)
XLA Ops:
  1.3 1.3 reshape.46.bin_ref
  2.6 160.5 %layer.1 = (f32[2,192,1024]{2,1,0:T(8,128)}, f32[2,192,1024]{2,1,0:T(8,128)}, bf16[768,768]{1,0:T(8,128)(2,1)}, bf16[768,768]{1,0:T(8,128)(2,1)}, f32[8,192]{1,0:T(8,128)}, /*index=5*/f32[1,768]{1,0:T(1,128)}) custom-call(f32[2,192,1024]{2,1,0:T(8,128)} %x_hbm.1, f32[2,192,1024]{2,1,0:T(8,128)} %cot_hbm.1, f32[768,768]{1,0:T(8,128)} %w1_hbm.1, ...), custom_call_target="tpu_custom_call" | custom-call | tf_op jit(solution)/shard_map/layer/pallas_call | solution.py:1093
  163.1 1.3 reduce
  164.3 1.5 fusion
  165.8 0.0 copy-start.2
  165.8 2.9 %convert_element_type.6 = f32[768,768]{1,0:T(8,128)} convert(bf16[768,768]{1,0:T(8,128)(2,1)} %get-tuple-element.19) | non-fusion elementwise | flops 589824 | bytes 3538944 | tf_op jit(solution)/shard_map/convert_element_type | solution.py:1109
  168.7 0.0 copy-done.2
  168.7 0.0 copy-start.1
  168.7 1.6 convert_element_type.7
  170.3 0.5 copy-done.1
  170.9 0.0 copy-start
  170.9 1.1 copy.28
  172.0 0.8 copy-done
  172.8 1.1 copy.29
Async XLA Ops:
  165.8 2.9 %copy-start.2 = (bf16[768,768]{1,0:T(8,128)(2,1)S(1)}, bf16[768,768]{1,0:T(8,128)(2,1)}, u32[]{:S(2)}) copy-start(bf16[768,768]{1,0:T(8,128)(2,1)} %get-tuple-element.21) | copy-start | bytes 3538948
  168.7 2.1 %copy-start.1 = (f32[2,192,1024]{2,1,0:T(8,128)S(1)}, f32[2,192,1024]{2,1,0:T(8,128)}, u32[]{:S(2)}) copy-start(f32[2,192,1024]{2,1,0:T(8,128)} %get-tuple-element.37) | copy-start | bytes 4718596
  170.9 2.0 %copy-start = (f32[2,192,1024]{2,1,0:T(8,128)S(1)}, f32[2,192,1024]{2,1,0:T(8,128)}, u32[]{:S(2)}) copy-start(f32[2,192,1024]{2,1,0:T(8,128)} %get-tuple-element.38) | copy-start | bytes 4718596

commit v2 on v1

--- a/solution.py
+++ b/solution.py
@@ -84,18 +84,32 @@
         self.ydev, self.zdev = self.flip[:2]
 
 
+class Fetch:
+    def __init__(self, made, place, free):
+        self.made, self.place, self.free = made, place, free
+
+    def wait(self):
+        self.made.wait()
+        self.free.append(self.place)
+
+
 class Links:
     def __init__(self, send, recv, near):
         self.send, self.recv, self.near = send, recv, near
-        self.used, self.fetched, self.open = 0, 0, []
+        self.used, self.sends, self.fetched = 0, 0, 0
+        self.free_sends, self.free_near, self.open = [], [], []
 
     def describe(self, src, dst, device):
         i = self.used
         self.used += 1
+        if not self.free_sends:
+            self.free_sends.append(self.sends)
+            self.sends += 1
+        self.place = self.free_sends.pop()
         return pltpu.make_async_remote_copy(
             src_ref=src,
             dst_ref=dst,
-            send_sem=self.send.at[i],
+            send_sem=self.send.at[self.place],
             recv_sem=self.recv.at[i],
             device_id=device,
             device_id_type=MESH,
@@ -104,22 +118,32 @@
     def copy(self, src, dst, device):
         made = self.describe(src, dst, device)
         made.start()
-        self.open.append(made)
+        self.open.append((made, self.place))
         return made
 
     def settle(self, some):
         for made in some:
-            made.wait_send()
-            self.drop(made)
-
-    def drop(self, made):
-        self.open = [other for other in self.open if other is not made]
+            for entry in self.open:
+                if entry[0] is made:
+                    made.wait_send()
+                    self.free_sends.append(entry[1])
+            self.open = [entry for entry in self.open if entry[0] is not made]
+
+    def settle_all(self):
+        self.settle([made for made, _ in self.open])
 
     def fetch(self, src, dst):
-        made = pltpu.make_async_copy(src, dst, self.near.at[self.fetched])
-        self.fetched += 1
-        made.start()
+        if not self.free_near:
+            self.free_near.append(self.fetched)
+            self.fetched += 1
+        place = self.free_near.pop()
+        made = Fetch(pltpu.make_async_copy(src, dst, self.near.at[place]), place, self.free_near)
+        made.made.start()
         return made
+
+
+def semaphores(bits):
+    return (94, 143, 34) if bits == 3 else (160, 192, 64)
 
 
 def greet(devices):
@@ -463,7 +487,7 @@
     g1_ref, s1_ref, bo_ref, g2_ref, s2_ref, bin_ref, live_ref,
     out_hbm, grad_hbm, wg1_hbm, wg2_hbm, light_ref, bias_ref,
     tab, small, ht, gt, order, xg, cs, ct, og, ab, sc, rc, sx, rx, acc, yf, hf, df, zf, u1, gr2, inv1, lanes,
-    wr, wt, wg, given, landing, ug, rowv, rows_in, pn, lsend, lrecv, lbias, ltot, lnext, send, recv, near,
+    wr, wt, wg, given, landing, ug, flat, rowv, rows_in, pn, lsend, lrecv, lbias, ltot, lnext, send, recv, near,
 ):
     slots, _, piece = x_hbm.shape
     parts, rows, tokens = cs.shape[1:]
@@ -539,10 +563,12 @@
 
     vectors = (g1_ref, s1_ref, bo_ref, g2_ref, s2_ref)
     rowv[...] = jnp.zeros_like(rowv)
+    for r in range(units // 128):
+        flat[:, r * 128 : (r + 1) * 128] = bin_ref[r : r + 1, :]
     for k, ref in enumerate(vectors):
         rowv[k : k + 1, 0:rows] = ref[...]
     for i in range(parts):
-        rowv[5 + i : 6 + i, 0:rows] = bin_ref[:, i * rows : (i + 1) * rows]
+        rowv[5 + i : 6 + i, 0:rows] = flat[:, i * rows : (i + 1) * rows]
     params = [links.copy(rowv, rows_in.at[me.h], device) for device in (me.core, me.side, me.cross)]
 
     small_in.wait()
@@ -850,6 +876,7 @@
 
     for made in seconds:
         made.wait_recv()
+    links.settle_all()
 
     def backward(s):
         backward_in(s, me.c, s == 0)
@@ -1038,11 +1065,12 @@
         ltot[bits] = ltot[k] + lnext[k]
     light_ref[...] = ltot[bits, 0:8]
     for i in range(parts):
-        bias_ref[:, i * rows : (i + 1) * rows] = ltot[bits, 8 + i : 9 + i]
+        flat[:, i * rows : (i + 1) * rows] = ltot[bits, 8 + i : 9 + i]
+    for r in range(units // 128):
+        bias_ref[r : r + 1, :] = flat[:, r * 128 : (r + 1) * 128]
     for made in stored:
         made.wait()
-    for made in list(links.open):
-        made.wait_send()
+    links.settle_all()
 
 
 def local(
@@ -1083,12 +1111,12 @@
         ((slots, 1, tokens), F32), ((7, HOLD, rows, 128), F32),
         ((2, 2, units, width), LOW), ((2, 2, width, units), LOW), ((2, units, width), F32),
         ((2, units, width), LOW), ((2, landing, width), LOW),
-        ((slots, SPLIT, pad, piece), LOW), ((16, 256), F32), ((HOLD, 16, 256), F32), ((HOLD, rows, 128), F32), ((HOLD, 8, rows), F32),
+        ((slots, SPLIT, pad, piece), LOW), ((1, units), F32), ((16, 256), F32), ((HOLD, 16, 256), F32), ((HOLD, rows, 128), F32), ((HOLD, 8, rows), F32),
         ((HOLD, 8, rows), F32), ((3, 8, rows), F32), ((bits + 1, 16, rows), F32), ((bits, 16, rows), F32),
     ]
     outs = [
         (layer_input.shape, F32), (layer_input.shape, F32), ((width, units), LOW), ((units, width), LOW),
-        ((8, rows), F32), ((1, units), F32),
+        ((8, rows), F32), ((units // 128, 128), F32),
     ]
     out, grad, wg1, wg2, light, bias = pl.pallas_call(
         functools.partial(layer_kernel, bits),
@@ -1097,13 +1125,13 @@
         in_specs=[any_] * 8 + [vmem] * 6 + [pl.BlockSpec(memory_space=pltpu.SMEM)],
         out_specs=[any_] * 4 + [vmem] * 2,
         scratch_shapes=[pltpu.VMEM(shape, kind) for shape, kind in scratch]
-        + [pltpu.SemaphoreType.DMA((192,)), pltpu.SemaphoreType.DMA((192,)), pltpu.SemaphoreType.DMA((96,))],
+        + [pltpu.SemaphoreType.DMA((count,)) for count in semaphores(bits)],
         compiler_params=pltpu.CompilerParams(
             collective_id=1, has_side_effects=True, vmem_limit_bytes=VMEM_LIMIT
         ),
     )(
         layer_input, cotangent, weight_in, weight_out, jnp.asarray(small), jnp.asarray(forward),
-        jnp.asarray(backward), jnp.asarray(order), *(v.reshape(1, -1) for v in vectors), live_counts,
+        jnp.asarray(backward), jnp.asarray(order), *(v.reshape(1, -1) for v in vectors[:5]), bias_in.reshape(-1, 128), live_counts,
     )
     return (
         out, grad, light[3], light[4], wg1.astype(F32), bias.reshape(units), wg2.astype(F32),

time: 174 us -> 171 us (0.983)
    unnamed x8 -> x11, local copies, waits for them, and re-layouts: 3.66 us -> 4.26 us
where the time goes in v2:
time: 171 us; the launch traced here: 170 us
  Pallas kernels  159 us (93%)
  local copies, waits for them, and re-layouts  5.72 us (3%)
  other arithmetic  4.52 us (3%)
    pallas_call x1, Pallas kernels, local(): pl.pallas_call(functools.partial(layer_kernel, bits), name='layer', out_s...  159 us
    unnamed x11, local copies, waits for them, and re-layouts  4.26 us

profile of v2, /device:TPU:0, one launch (start us, length us, event | category | flops | bytes accessed | tf_op | source)
XLA Modules:
  0.0 170.3 jit_solution(11274283808634343153)
XLA Ops:
  1.3 158.8 %layer.1 = (f32[2,192,1024]{2,1,0:T(8,128)}, f32[2,192,1024]{2,1,0:T(8,128)}, bf16[768,768]{1,0:T(8,128)(2,1)}, bf16[768,768]{1,0:T(8,128)(2,1)}, f32[8,192]{1,0:T(8,128)}, /*index=5*/f32[6,128]{1,0:T(8,128)}) custom-call(f32[2,192,1024]{2,1,0:T(8,128)} %x_hbm.1, f32[2,192,1024]{2,1,0:T(8,128)} %cot_hbm.1, f32[768,768]{1,0:T(8,128)} %w1_hbm.1, ...), custom_call_target="tpu_custom_call" | custom-call | tf_op jit(solution)/shard_map/layer/pallas_call | solution.py:1121
  160.1 1.5 fusion
  161.5 0.0 copy-start.2
  161.6 2.9 %convert_element_type.6 = f32[768,768]{1,0:T(8,128)} convert(bf16[768,768]{1,0:T(8,128)(2,1)} %get-tuple-element.19) | non-fusion elementwise | flops 589824 | bytes 3538944 | tf_op jit(solution)/shard_map/convert_element_type | solution.py:1137
  164.5 0.0 copy-done.2
  164.5 0.0 copy-start.1
  164.5 1.6 convert_element_type.7
  166.1 0.5 copy-done.1
  166.6 0.0 copy-start
  166.6 1.1 copy.29
  167.8 0.8 copy-done
  168.6 0.0 copy-start.3
  168.6 1.1 copy.30
  169.7 0.0 copy-done.3
  169.7 0.6 copy.31
Async XLA Ops:
  161.5 2.9 %copy-start.2 = (bf16[768,768]{1,0:T(8,128)(2,1)S(1)}, bf16[768,768]{1,0:T(8,128)(2,1)}, u32[]{:S(2)}) copy-start(bf16[768,768]{1,0:T(8,128)(2,1)} %get-tuple-element.21) | copy-start | bytes 3538948
  164.5 2.1 %copy-start.1 = (f32[2,192,1024]{2,1,0:T(8,128)S(1)}, f32[2,192,1024]{2,1,0:T(8,128)}, u32[]{:S(2)}) copy-start(f32[2,192,1024]{2,1,0:T(8,128)} %get-tuple-element.37) | copy-start | bytes 4718596
  166.6 2.0 %copy-start = (f32[2,192,1024]{2,1,0:T(8,128)S(1)}, f32[2,192,1024]{2,1,0:T(8,128)}, u32[]{:S(2)}) copy-start(f32[2,192,1024]{2,1,0:T(8,128)} %get-tuple-element.38) | copy-start | bytes 4718596
  168.6 1.1 copy-start.3

commit v3 on v2

--- a/solution.py
+++ b/solution.py
@@ -143,7 +143,7 @@
 
 
 def semaphores(bits):
-    return (94, 143, 34) if bits == 3 else (160, 192, 64)
+    return (47, 143, 34) if bits == 3 else (160, 192, 64)
 
 
 def greet(devices):
@@ -309,6 +309,7 @@
     def add(self, made, mine, place):
         made.wait_recv()
         self.add_rows(mine, self.landing, place.start)
+        self.links.settle([made])
 
     def add_rows(self, mine, landing, start):
         def some(at, i, step):
@@ -334,6 +335,7 @@
         def after():
             made.wait_recv()
             self.add_rows(mine, self.given_landing, place.start)
+            self.links.settle([made])
 
         self.after = after
 
@@ -358,6 +360,7 @@
                     self.given[rows, :] = total.astype(LOW)
 
                 by_rows(keep, half, some)
+                self.links.settle([far])
             self.add(made, mine, place)
 
         self.after = after
@@ -404,6 +407,7 @@
         def after():
             for one in made:
                 one.wait_recv()
+            self.links.settle(made)
 
         self.after = after
 

time: 171 us -> 170 us (level)
  no operation moved by 1% of the time
where the time goes in v3:
time: 170 us
  Pallas kernels  158 us (93%)
  local copies, waits for them, and re-layouts  5.72 us (3%)
  other arithmetic  4.52 us (3%)
    pallas_call x1, Pallas kernels, local(): pl.pallas_call(functools.partial(layer_kernel, bits), name='layer', out_s...  158 us
    unnamed x11, local copies, waits for them, and re-layouts  4.26 us

profile of v3, /device:TPU:0, one launch (start us, length us, event | category | flops | bytes accessed | tf_op | source)
XLA Modules:
  0.0 169.8 jit_solution(3053562832365348431)
XLA Ops:
  1.3 158.3 %layer.1 = (f32[2,192,1024]{2,1,0:T(8,128)}, f32[2,192,1024]{2,1,0:T(8,128)}, bf16[768,768]{1,0:T(8,128)(2,1)}, bf16[768,768]{1,0:T(8,128)(2,1)}, f32[8,192]{1,0:T(8,128)}, /*index=5*/f32[6,128]{1,0:T(8,128)}) custom-call(f32[2,192,1024]{2,1,0:T(8,128)} %x_hbm.1, f32[2,192,1024]{2,1,0:T(8,128)} %cot_hbm.1, f32[768,768]{1,0:T(8,128)} %w1_hbm.1, ...), custom_call_target="tpu_custom_call" | custom-call | tf_op jit(solution)/shard_map/layer/pallas_call | solution.py:1125
  159.6 1.5 fusion
  161.1 0.0 copy-start.2
  161.1 2.9 %convert_element_type.6 = f32[768,768]{1,0:T(8,128)} convert(bf16[768,768]{1,0:T(8,128)(2,1)} %get-tuple-element.19) | non-fusion elementwise | flops 589824 | bytes 3538944 | tf_op jit(solution)/shard_map/convert_element_type | solution.py:1141
  164.0 0.0 copy-done.2
  164.0 0.0 copy-start.1
  164.0 1.6 convert_element_type.7
  165.6 0.5 copy-done.1
  166.1 0.0 copy-start
  166.1 1.1 copy.29
  167.3 0.8 copy-done
  168.1 0.0 copy-start.3
  168.1 1.1 copy.30
  169.2 0.0 copy-done.3
  169.2 0.6 copy.31
Async XLA Ops:
  161.1 2.9 %copy-start.2 = (bf16[768,768]{1,0:T(8,128)(2,1)S(1)}, bf16[768,768]{1,0:T(8,128)(2,1)}, u32[]{:S(2)}) copy-start(bf16[768,768]{1,0:T(8,128)(2,1)} %get-tuple-element.21) | copy-start | bytes 3538948
  164.0 2.1 %copy-start.1 = (f32[2,192,1024]{2,1,0:T(8,128)S(1)}, f32[2,192,1024]{2,1,0:T(8,128)}, u32[]{:S(2)}) copy-start(f32[2,192,1024]{2,1,0:T(8,128)} %get-tuple-element.37) | copy-start | bytes 4718596
  166.1 2.0 %copy-start = (f32[2,192,1024]{2,1,0:T(8,128)S(1)}, f32[2,192,1024]{2,1,0:T(8,128)}, u32[]{:S(2)}) copy-start(f32[2,192,1024]{2,1,0:T(8,128)} %get-tuple-element.38) | copy-start | bytes 4718596
  168.1 1.1 copy-start.3

commit v4 on v3

--- a/solution.py
+++ b/solution.py
@@ -202,7 +202,7 @@
         self.me, self.links, self.rows, self.sent = me, links, rows, []
         self.sc, self.rc, self.sx, self.rx, self.acc = sc, rc, sx, rx, acc
 
-    def run(self, prepare, block, hook):
+    def run(self, prepare, block, hook, early=False):
         x, c, cut = self.me.x, self.me.c, pl.ds(0, self.rows)
         for n, start in enumerate((2 * (1 - x), 2 * x)):
             away, home = start + 1 - c, start + c
@@ -222,12 +222,15 @@
             by_core = self.links.copy(self.sc.at[n, :, cut], self.rc.at[n, :, cut], self.me.core)
             self.sent.append(by_core)
             prepare(1, home)
+            if n == 0 and early:
+                hook()
             by_core.wait_recv()
             block(1, home, keep)
             if n == 0:
                 self.by_side = self.links.copy(self.sx, self.rx, self.me.side)
                 self.sent.append(self.by_side)
-                hook()
+                if not early:
+                    hook()
 
     def wait(self):
         self.by_side.wait_recv()
@@ -636,7 +639,7 @@
         hand_over(s, me.pd)
         for made in over[s]:
             made.wait_recv()
-        sums[s].run(functools.partial(prepare, s), functools.partial(transform, s), hook)
+        sums[s].run(functools.partial(prepare, s), functools.partial(transform, s), hook, early=s == 0)
         for to, device in ((me.hc, me.core), (me.hx, me.side), (me.hd, me.cross)):
             moved.append(links.copy(cs.at[s, to], ct.at[s, me.h], device))
         links.settle(over[s] + spread[s].sent())

time: 170 us -> 170 us (level)
  no operation moved by 1% of the time
where the time goes in v4:
time: 170 us
  Pallas kernels  158 us (93%)
  local copies, waits for them, and re-layouts  5.72 us (3%)
  other arithmetic  4.52 us (3%)
    pallas_call x1, Pallas kernels, local(): pl.pallas_call(functools.partial(layer_kernel, bits), name='layer', out_s...  158 us
    unnamed x11, local copies, waits for them, and re-layouts  4.26 us

profile of v4, /device:TPU:0, one launch (start us, length us, event | category | flops | bytes accessed | tf_op | source)
XLA Modules:
  0.0 169.7 jit_solution(17186897701652123206)
XLA Ops:
  1.3 158.2 %layer.1 = (f32[2,192,1024]{2,1,0:T(8,128)}, f32[2,192,1024]{2,1,0:T(8,128)}, bf16[768,768]{1,0:T(8,128)(2,1)}, bf16[768,768]{1,0:T(8,128)(2,1)}, f32[8,192]{1,0:T(8,128)}, /*index=5*/f32[6,128]{1,0:T(8,128)}) custom-call(f32[2,192,1024]{2,1,0:T(8,128)} %x_hbm.1, f32[2,192,1024]{2,1,0:T(8,128)} %cot_hbm.1, f32[768,768]{1,0:T(8,128)} %w1_hbm.1, ...), custom_call_target="tpu_custom_call" | custom-call | tf_op jit(solution)/shard_map/layer/pallas_call | solution.py:1128
  159.5 1.5 fusion
  160.9 0.0 copy-start.2
  160.9 2.9 %convert_element_type.6 = f32[768,768]{1,0:T(8,128)} convert(bf16[768,768]{1,0:T(8,128)(2,1)} %get-tuple-element.19) | non-fusion elementwise | flops 589824 | bytes 3538944 | tf_op jit(solution)/shard_map/convert_element_type | solution.py:1144
  163.9 0.0 copy-done.2
  163.9 0.0 copy-start.1
  163.9 1.6 convert_element_type.7
  165.5 0.5 copy-done.1
  166.0 0.0 copy-start
  166.0 1.1 copy.29
  167.2 0.8 copy-done
  168.0 0.0 copy-start.3
  168.0 1.1 copy.30
  169.1 0.0 copy-done.3
  169.1 0.6 copy.31
Async XLA Ops:
  160.9 2.9 %copy-start.2 = (bf16[768,768]{1,0:T(8,128)(2,1)S(1)}, bf16[768,768]{1,0:T(8,128)(2,1)}, u32[]{:S(2)}) copy-start(bf16[768,768]{1,0:T(8,128)(2,1)} %get-tuple-element.21) | copy-start | bytes 3538948
  163.9 2.1 %copy-start.1 = (f32[2,192,1024]{2,1,0:T(8,128)S(1)}, f32[2,192,1024]{2,1,0:T(8,128)}, u32[]{:S(2)}) copy-start(f32[2,192,1024]{2,1,0:T(8,128)} %get-tuple-element.37) | copy-start | bytes 4718596
  166.0 2.0 %copy-start = (f32[2,192,1024]{2,1,0:T(8,128)S(1)}, f32[2,192,1024]{2,1,0:T(8,128)}, u32[]{:S(2)}) copy-start(f32[2,192,1024]{2,1,0:T(8,128)} %get-tuple-element.38) | copy-start | bytes 4718596
  168.0 1.1 copy-start.3
